TPU v7x, 256 devices: a whole 4x4x8 slice. The times are simulated.
256 devices in a mesh: gen: 32 (over y, x, core), beam: 8 (over z).
Axes of the slice: x: 4, y: 4, z: 8, core: 2. Of those that a mesh axis runs over, the one named last changes fastest.
Arguments:
- gen_showers: bfloat16 [32768, 256], P('gen'), may hold values from -12 to 12
- beam_showers: bfloat16 [16384, 256], P('beam'), may hold values from -6 to 6
- embed_weight: bfloat16 [256, 128], replicated, may hold values from -0.375 to 0.375
- eps_roster: float32 [4], replicated, may hold values from 0.04 to 0.08
Outputs:
- gen_potential: float32 [32768], P('gen')
- beam_potential: float32 [16384], P('beam')
- weight_grad: float32 [256, 128], replicated
All inputs are finite; a program needn't handle non-finite values.
Results may differ from a plain program's by a relative error of at most 0.03.
Values sent between devices are 32-bit elements; how exact they have to be, the bound alone decides.
No kernel may reach another device: no remote copies, remote signals or barrier semaphores. Data moves between devices by JAX's collectives and lax.ppermute only.
A program may use at most 64 MiB of HBM per device.

v0:
```python
import math
import jax
import jax.numpy as jnp
from jax import lax
from jax.sharding import PartitionSpec as P

SWEEPS = 4


def embed(showers, weight):
    act = jnp.tanh(jnp.dot(showers, weight, preferred_element_type=jnp.float32))
    return (act, act.astype(jnp.bfloat16))


def tile_cost(gen_emb, beam_emb, gen_sq, beam_sq):
    cross = lax.dot_general(
        gen_emb, beam_emb, (((1,), (1,)), ((), ())), preferred_element_type=jnp.float32
    )
    return gen_sq[:, None] + beam_sq[None, :] - 2.0 * cross


def row_lse(scores):
    top = lax.pmax(jnp.max(scores, axis=1), "beam")
    total = lax.psum(jnp.sum(jnp.exp(scores - top[:, None]), axis=1), "beam")
    return top + jnp.log(total)


def col_lse(scores):
    top = lax.pmax(jnp.max(scores, axis=0), "gen")
    total = lax.psum(jnp.sum(jnp.exp(scores - top[None, :]), axis=0), "gen")
    return top + jnp.log(total)


def transpose_dot(left, right):
    return lax.dot_general(
        left.astype(jnp.float32),
        right,
        (((0,), (0,)), ((), ())),
        precision=lax.Precision.HIGHEST,
        preferred_element_type=jnp.float32,
    )


def on_device(gen_showers, beam_showers, embed_weight, eps_roster):
    gen_act, gen_emb = embed(gen_showers, embed_weight)
    beam_act, beam_emb = embed(beam_showers, embed_weight)
    gen_float = gen_emb.astype(jnp.float32)
    beam_float = beam_emb.astype(jnp.float32)
    gen_sq = jnp.sum(gen_float * gen_float, axis=1)
    beam_sq = jnp.sum(beam_float * beam_float, axis=1)
    rows = gen_emb.shape[0]
    columns = beam_emb.shape[0]
    log_beam = math.log(columns * lax.axis_size("beam"))
    log_gen = math.log(rows * lax.axis_size("gen"))
    beam_pot = jnp.zeros((columns,), jnp.float32)
    gen_pot = jnp.zeros((rows,), jnp.float32)
    for sweep in range(SWEEPS):
        temper = eps_roster[sweep]
        cost = tile_cost(gen_emb, beam_emb, gen_sq, beam_sq)
        gen_pot = temper * (log_beam - row_lse((beam_pot[None, :] - cost) / temper))
        cost = tile_cost(gen_emb, beam_emb, gen_sq, beam_sq)
        beam_pot = temper * (log_gen - col_lse((gen_pot[:, None] - cost) / temper))
    last = eps_roster[SWEEPS - 1]
    cost = tile_cost(gen_emb, beam_emb, gen_sq, beam_sq)
    mass = jnp.exp((gen_pot[:, None] + beam_pot[None, :] - cost) / last - log_beam)
    plan = mass.astype(jnp.bfloat16)
    gen_count = rows // lax.axis_size("beam")
    part = plan
    row_mass = jnp.sum(mass, axis=1)
    own = gen_float
    moved = jnp.dot(part, beam_emb, preferred_element_type=jnp.float32)
    grad_gen = lax.psum_scatter(
        2.0 * (row_mass[:, None] * own - moved), "beam", scatter_dimension=0, tiled=True
    )
    gen_start = lax.axis_index("beam") * gen_count
    act_rows = lax.dynamic_slice_in_dim(gen_act, gen_start, gen_count, 0)
    shower_rows = lax.dynamic_slice_in_dim(gen_showers, gen_start, gen_count, 0)
    beam_count = columns // lax.axis_size("gen")
    part = plan
    col_mass = jnp.sum(mass, axis=0)
    own = beam_float
    moved = lax.dot_general(
        part, gen_emb, (((0,), (0,)), ((), ())), preferred_element_type=jnp.float32
    )
    grad_beam = lax.psum_scatter(
        2.0 * (col_mass[:, None] * own - moved), "gen", scatter_dimension=0, tiled=True
    )
    beam_start = lax.axis_index("gen") * beam_count
    act_cols = lax.dynamic_slice_in_dim(beam_act, beam_start, beam_count, 0)
    shower_cols = lax.dynamic_slice_in_dim(beam_showers, beam_start, beam_count, 0)
    partial_grad = transpose_dot(shower_rows, grad_gen * (1.0 - act_rows * act_rows))
    partial_grad = partial_grad + transpose_dot(
        shower_cols, grad_beam * (1.0 - act_cols * act_cols)
    )
    weight_grad = lax.psum(partial_grad, ("gen", "beam"))
    return (gen_pot, beam_pot, weight_grad)


def solution(mesh):
    in_specs = (P("gen", None), P("beam", None), P(), P())
    out_specs = (P("gen"), P("beam"), P())
    return jax.shard_map(
        on_device, mesh=mesh, in_specs=in_specs, out_specs=out_specs, check_vma=False
    )
```

profile of v0, /device:TPU:8, one launch (start us, length us, event | category | flops | bytes accessed | tf_op | source)
XLA Modules:
  0.0 1114.6 jit_solution(14821040143072383777)
XLA Ops:
  11.4 5.3 fusion
  16.7 20.0 %pmax.56 = f32[1024]{0:T(1024)S(1)} all-reduce(f32[1024]{0:T(1024)S(1)} %get-tuple-element.16), channel_id=1, replica_groups=mesh['gen'=32,'beam'=8] {'beam'}, use_global_device_ids=true, to_apply=%region_3.0 | all-reduce | flops 1024 | bytes 8192 | tf_op jit(solution)/shard_map/pmax | solution.py:23
  41.8 14.2 %psum.63 = f32[1024]{0:T(1024)S(1)} all-reduce(f32[1024]{0:T(1024)S(1)} %exponential_reduce_fusion.7), channel_id=1, replica_groups=mesh['gen'=32,'beam'=8] {'beam'}, use_global_device_ids=true, to_apply=%region_5.0 | all-reduce | flops 1024 | bytes 8192 | tf_op jit(solution)/shard_map/psum | solution.py:24
  61.3 54.0 %pmax.57 = f32[2048]{0:T(1024)S(1)} all-reduce(f32[2048]{0:T(1024)S(1)} %fusion.15), channel_id=1, replica_groups=mesh['gen'=32,'beam'=8] {'gen'}, use_global_device_ids=true, to_apply=%region_7.0 | all-reduce | flops 2048 | bytes 16384 | tf_op jit(solution)/shard_map/pmax | solution.py:29
  115.4 5.2 exponential_reduce_fusion.6
  120.5 55.5 %psum.64 = f32[2048]{0:T(1024)S(1)} all-reduce(f32[2048]{0:T(1024)S(1)} %exponential_reduce_fusion.6), channel_id=1, replica_groups=mesh['gen'=32,'beam'=8] {'gen'}, use_global_device_ids=true, to_apply=%region_9.0 | all-reduce | flops 2048 | bytes 16384 | tf_op jit(solution)/shard_map/psum | solution.py:30
  181.5 16.2 %pmax.58 = f32[1024]{0:T(1024)S(1)} all-reduce(f32[1024]{0:T(1024)S(1)} %fusion.1), channel_id=1, replica_groups=mesh['gen'=32,'beam'=8] {'beam'}, use_global_device_ids=true, to_apply=%region_11.0 | all-reduce | flops 1024 | bytes 8192 | tf_op jit(solution)/shard_map/pmax | solution.py:23
  202.8 14.2 %psum.65 = f32[1024]{0:T(1024)S(1)} all-reduce(f32[1024]{0:T(1024)S(1)} %exponential_reduce_fusion.5), channel_id=1, replica_groups=mesh['gen'=32,'beam'=8] {'beam'}, use_global_device_ids=true, to_apply=%region_13.0 | all-reduce | flops 1024 | bytes 8192 | tf_op jit(solution)/shard_map/psum | solution.py:24
  222.1 63.7 %pmax.59 = f32[2048]{0:T(1024)S(1)} all-reduce(f32[2048]{0:T(1024)S(1)} %fusion.16), channel_id=1, replica_groups=mesh['gen'=32,'beam'=8] {'gen'}, use_global_device_ids=true, to_apply=%region_15.0 | all-reduce | flops 2048 | bytes 16384 | tf_op jit(solution)/shard_map/pmax | solution.py:29
  290.9 63.7 %psum.66 = f32[2048]{0:T(1024)S(1)} all-reduce(f32[2048]{0:T(1024)S(1)} %exponential_reduce_fusion.4), channel_id=1, replica_groups=mesh['gen'=32,'beam'=8] {'gen'}, use_global_device_ids=true, to_apply=%region_17.0 | all-reduce | flops 2048 | bytes 16384 | tf_op jit(solution)/shard_map/psum | solution.py:30
  360.1 16.2 %pmax.60 = f32[1024]{0:T(1024)S(1)} all-reduce(f32[1024]{0:T(1024)S(1)} %fusion.2), channel_id=1, replica_groups=mesh['gen'=32,'beam'=8] {'beam'}, use_global_device_ids=true, to_apply=%region_19.0 | all-reduce | flops 1024 | bytes 8192 | tf_op jit(solution)/shard_map/pmax | solution.py:23
  381.4 14.3 %psum.67 = f32[1024]{0:T(1024)S(1)} all-reduce(f32[1024]{0:T(1024)S(1)} %exponential_reduce_fusion.3), channel_id=1, replica_groups=mesh['gen'=32,'beam'=8] {'beam'}, use_global_device_ids=true, to_apply=%region_21.0 | all-reduce | flops 1024 | bytes 8192 | tf_op jit(solution)/shard_map/psum | solution.py:24
  401.1 63.7 %pmax.61 = f32[2048]{0:T(1024)S(1)} all-reduce(f32[2048]{0:T(1024)S(1)} %fusion.17), channel_id=1, replica_groups=mesh['gen'=32,'beam'=8] {'gen'}, use_global_device_ids=true, to_apply=%region_23.0 | all-reduce | flops 2048 | bytes 16384 | tf_op jit(solution)/shard_map/pmax | solution.py:29
  464.8 5.2 exponential_reduce_fusion.2
  470.0 63.7 %psum.68 = f32[2048]{0:T(1024)S(1)} all-reduce(f32[2048]{0:T(1024)S(1)} %exponential_reduce_fusion.2), channel_id=1, replica_groups=mesh['gen'=32,'beam'=8] {'gen'}, use_global_device_ids=true, to_apply=%region_25.0 | all-reduce | flops 2048 | bytes 16384 | tf_op jit(solution)/shard_map/psum | solution.py:30
  539.2 16.2 %pmax.62 = f32[1024]{0:T(1024)S(1)} all-reduce(f32[1024]{0:T(1024)S(1)} %fusion.3), channel_id=1, replica_groups=mesh['gen'=32,'beam'=8] {'beam'}, use_global_device_ids=true, to_apply=%region_27.0 | all-reduce | flops 1024 | bytes 8192 | tf_op jit(solution)/shard_map/pmax | solution.py:23
  560.5 14.2 %psum.69 = f32[1024]{0:T(1024)S(1)} all-reduce(f32[1024]{0:T(1024)S(1)} %exponential_reduce_fusion.1), channel_id=1, replica_groups=mesh['gen'=32,'beam'=8] {'beam'}, use_global_device_ids=true, to_apply=%region_29.0 | all-reduce | flops 1024 | bytes 8192 | tf_op jit(solution)/shard_map/psum | solution.py:24
  580.0 63.7 %pmax.63 = f32[2048]{0:T(1024)S(1)} all-reduce(f32[2048]{0:T(1024)S(1)} %fusion.18), channel_id=1, replica_groups=mesh['gen'=32,'beam'=8] {'gen'}, use_global_device_ids=true, to_apply=%region_31.0 | all-reduce | flops 2048 | bytes 16384 | tf_op jit(solution)/shard_map/pmax | solution.py:29
  643.7 5.2 exponential_reduce_fusion
  648.9 63.7 %psum.70 = f32[2048]{0:T(1024)S(1)} all-reduce(f32[2048]{0:T(1024)S(1)} %exponential_reduce_fusion), channel_id=1, replica_groups=mesh['gen'=32,'beam'=8] {'gen'}, use_global_device_ids=true, to_apply=%region_33.0 | all-reduce | flops 2048 | bytes 16384 | tf_op jit(solution)/shard_map/psum | solution.py:30
  713.3 5.7 fusion.37
  728.0 92.3 %reduce-scatter.5.cloned.1.call-done = f32[64,128]{1,0:T(8,128)} async-done(((f32[2048,128]{1,0:T(8,128)}), f32[64,128]{1,0:T(8,128)}) %reduce-scatter.5.cloned.1.call-update) | async-done | bytes 32784 | tf_op jit(solution)/shard_map/reduce_scatter | solution.py:85
  821.3 38.7 %reduce-scatter.3.cloned.1.call-done = f32[128,128]{0,1:T(8,128)} async-done(((f32[1024,128]{0,1:T(8,128)}), f32[128,128]{0,1:T(8,128)}) %reduce-scatter.3.cloned.1.call-update) | async-done | bytes 65552 | tf_op jit(solution)/shard_map/reduce_scatter | solution.py:72
  861.7 244.8 %all-reduce.2.cloned.1.call-done = f32[256,128]{1,0:T(8,128)} async-done(((f32[256,128]{1,0:T(8,128)}), f32[256,128]{1,0:T(8,128)}) %all-reduce.2.cloned.1.call-update) | async-done | bytes 131088 | tf_op jit(solution)/shard_map/psum | solution.py:95
  (42 shorter events, 81.4 us)
Async XLA Ops:
  7.2 1.5 copy-start
  7.2 813.0 %reduce-scatter.5.cloned.1.call-start = ((), (), s32[]{:S(2)}) async-start(), calls=%async_computation.3 | async-start | bytes 1081344 | tf_op jit(solution)/shard_map/reduce_scatter | solution.py:85
  575.4 137.9 %copy-start.2 = (f32[1024]{0:T(1024)}, f32[1024]{0:T(1024)S(1)}, u32[]{:S(2)}) copy-start(f32[1024]{0:T(1024)S(1)} %subtract_multiply_fusion.4) | copy-start | bytes 12292
  713.3 10.0 copy-start.3
  719.0 1.9 copy-start.1
  723.3 136.6 %reduce-scatter.3.cloned.1.call-start = ((), (), s32[]{:S(2)}) async-start(), calls=%async_computation.2 | async-start | bytes 589824 | tf_op jit(solution)/shard_map/reduce_scatter | solution.py:72
  727.9 378.6 %all-reduce.2.cloned.1.call-start = ((), (), s32[]{:S(2)}) async-start(), calls=%async_computation.4 | async-start | bytes 262144 | tf_op jit(solution)/shard_map/psum | solution.py:95
Sparse Core Ops, SparseCore 0:
  723.5 96.7 reduce-scatter.4
  822.9 36.9 reduce-scatter.2
  866.0 240.4 all-reduce.1
where the time goes:
time: 1120 us; the launch traced here: 1110 us
  blocking collectives  617 us (55%)
  waiting for transfers between devices  376 us (34%)
  other arithmetic  85 us (8%)
  matrix products  17.8 us (2%)
  between operations  14 us (1%)
    psum x4, blocking collectives, col_lse(): total = lax.psum(jnp.sum(jnp.exp(scores - top[None, :]), axis=0), 'gen')  247 us
    pmax x4, blocking collectives, col_lse(): top = lax.pmax(jnp.max(scores, axis=0), 'gen')  245 us
    psum x1, waiting for transfers between devices, on_device(): weight_grad = lax.psum(partial_grad, ('gen', 'beam'))  245 us
    reduce_scatter x1, waiting for transfers between devices, on_device(): lax.psum_scatter(2.0 * (col_mass[:, None] * own - moved), 'gen', scatter_...  92.3 us
    pmax x4, blocking collectives, row_lse(): top = lax.pmax(jnp.max(scores, axis=1), 'beam')  68.5 us
    psum x4, blocking collectives, row_lse(): total = lax.psum(jnp.sum(jnp.exp(scores - top[:, None]), axis=1), 'beam')  56.8 us
    reduce_scatter x1, waiting for transfers between devices, on_device(): lax.psum_scatter(2.0 * (row_mass[:, None] * own - moved), 'beam', scatter...  38.7 us
  transfers between devices with their start and end apart: 3, of which 3 were waited for; matrix products, arithmetic and copies ran while one was open for 0% of the time, Pallas kernels for 0%

commit v1 on v0

--- a/solution.py
+++ b/solution.py
@@ -92,7 +92,13 @@
     partial_grad = partial_grad + transpose_dot(
         shower_cols, grad_beam * (1.0 - act_cols * act_cols)
     )
-    weight_grad = lax.psum(partial_grad, ("gen", "beam"))
+
+    def treat_node(state):
+        for k0 in ("gen", "beam"):
+            state = lax.psum(state, k0)
+        return state
+
+    weight_grad = treat_node(partial_grad)
     return (gen_pot, beam_pot, weight_grad)
 
 

time: 1120 us -> 1060 us (0.946)
  waiting for transfers between devices: 376 us -> 315 us
    psum x1 -> x2, waiting for transfers between devices: 245 us -> 184 us  [treat_node(): state = lax.psum(state, k0)]
  transfers between devices with their start and end apart: 3 -> 4, of which waited for: 3 -> 4; matrix products, arithmetic and copies ran while one was open for 0% -> 1% of each run, Pallas kernels for 0% -> 0%
where the time goes in v1:
time: 1060 us; the launch traced here: 1050 us
  blocking collectives  617 us (58%)
  waiting for transfers between devices  315 us (30%)
  other arithmetic  85 us (8%)
  matrix products  17.8 us (2%)
  between operations  14 us (1%)
    psum x4, blocking collectives, col_lse(): total = lax.psum(jnp.sum(jnp.exp(scores - top[None, :]), axis=0), 'gen')  247 us
    pmax x4, blocking collectives, col_lse(): top = lax.pmax(jnp.max(scores, axis=0), 'gen')  245 us
    psum x2, waiting for transfers between devices, treat_node(): state = lax.psum(state, k0)  184 us
    reduce_scatter x1, waiting for transfers between devices, on_device(): lax.psum_scatter(2.0 * (col_mass[:, None] * own - moved), 'gen', scatter_...  92.3 us
    pmax x4, blocking collectives, row_lse(): top = lax.pmax(jnp.max(scores, axis=1), 'beam')  68.5 us
    psum x4, blocking collectives, row_lse(): total = lax.psum(jnp.sum(jnp.exp(scores - top[:, None]), axis=1), 'beam')  56.8 us
    reduce_scatter x1, waiting for transfers between devices, on_device(): lax.psum_scatter(2.0 * (row_mass[:, None] * own - moved), 'beam', scatter...  38.7 us
  transfers between devices with their start and end apart: 4, of which 4 were waited for; matrix products, arithmetic and copies ran while one was open for 1% of the time, Pallas kernels for 0%

profile of v1, /device:TPU:8, one launch (start us, length us, event | category | flops | bytes accessed | tf_op | source)
XLA Modules:
  0.0 1054.3 jit_solution(7304851526449598381)
XLA Ops:
  11.4 5.3 fusion
  16.7 20.0 %pmax.56 = f32[1024]{0:T(1024)S(1)} all-reduce(f32[1024]{0:T(1024)S(1)} %get-tuple-element.16), channel_id=1, replica_groups=mesh['gen'=32,'beam'=8] {'beam'}, use_global_device_ids=true, to_apply=%region_3.0 | all-reduce | flops 1024 | bytes 8192 | tf_op jit(solution)/shard_map/pmax | solution.py:23
  41.8 14.2 %psum.70 = f32[1024]{0:T(1024)S(1)} all-reduce(f32[1024]{0:T(1024)S(1)} %exponential_reduce_fusion.7), channel_id=1, replica_groups=mesh['gen'=32,'beam'=8] {'beam'}, use_global_device_ids=true, to_apply=%region_5.0 | all-reduce | flops 1024 | bytes 8192 | tf_op jit(solution)/shard_map/psum | solution.py:24
  61.3 54.0 %pmax.57 = f32[2048]{0:T(1024)S(1)} all-reduce(f32[2048]{0:T(1024)S(1)} %fusion.15), channel_id=1, replica_groups=mesh['gen'=32,'beam'=8] {'gen'}, use_global_device_ids=true, to_apply=%region_7.0 | all-reduce | flops 2048 | bytes 16384 | tf_op jit(solution)/shard_map/pmax | solution.py:29
  115.4 5.2 exponential_reduce_fusion.6
  120.5 55.5 %psum.71 = f32[2048]{0:T(1024)S(1)} all-reduce(f32[2048]{0:T(1024)S(1)} %exponential_reduce_fusion.6), channel_id=1, replica_groups=mesh['gen'=32,'beam'=8] {'gen'}, use_global_device_ids=true, to_apply=%region_9.0 | all-reduce | flops 2048 | bytes 16384 | tf_op jit(solution)/shard_map/psum | solution.py:30
  181.5 16.2 %pmax.58 = f32[1024]{0:T(1024)S(1)} all-reduce(f32[1024]{0:T(1024)S(1)} %fusion.1), channel_id=1, replica_groups=mesh['gen'=32,'beam'=8] {'beam'}, use_global_device_ids=true, to_apply=%region_11.0 | all-reduce | flops 1024 | bytes 8192 | tf_op jit(solution)/shard_map/pmax | solution.py:23
  202.8 14.2 %psum.72 = f32[1024]{0:T(1024)S(1)} all-reduce(f32[1024]{0:T(1024)S(1)} %exponential_reduce_fusion.5), channel_id=1, replica_groups=mesh['gen'=32,'beam'=8] {'beam'}, use_global_device_ids=true, to_apply=%region_13.0 | all-reduce | flops 1024 | bytes 8192 | tf_op jit(solution)/shard_map/psum | solution.py:24
  222.1 63.7 %pmax.59 = f32[2048]{0:T(1024)S(1)} all-reduce(f32[2048]{0:T(1024)S(1)} %fusion.16), channel_id=1, replica_groups=mesh['gen'=32,'beam'=8] {'gen'}, use_global_device_ids=true, to_apply=%region_15.0 | all-reduce | flops 2048 | bytes 16384 | tf_op jit(solution)/shard_map/pmax | solution.py:29
  290.9 63.7 %psum.73 = f32[2048]{0:T(1024)S(1)} all-reduce(f32[2048]{0:T(1024)S(1)} %exponential_reduce_fusion.4), channel_id=1, replica_groups=mesh['gen'=32,'beam'=8] {'gen'}, use_global_device_ids=true, to_apply=%region_17.0 | all-reduce | flops 2048 | bytes 16384 | tf_op jit(solution)/shard_map/psum | solution.py:30
  360.1 16.2 %pmax.60 = f32[1024]{0:T(1024)S(1)} all-reduce(f32[1024]{0:T(1024)S(1)} %fusion.2), channel_id=1, replica_groups=mesh['gen'=32,'beam'=8] {'beam'}, use_global_device_ids=true, to_apply=%region_19.0 | all-reduce | flops 1024 | bytes 8192 | tf_op jit(solution)/shard_map/pmax | solution.py:23
  381.4 14.3 %psum.74 = f32[1024]{0:T(1024)S(1)} all-reduce(f32[1024]{0:T(1024)S(1)} %exponential_reduce_fusion.3), channel_id=1, replica_groups=mesh['gen'=32,'beam'=8] {'beam'}, use_global_device_ids=true, to_apply=%region_21.0 | all-reduce | flops 1024 | bytes 8192 | tf_op jit(solution)/shard_map/psum | solution.py:24
  401.1 63.7 %pmax.61 = f32[2048]{0:T(1024)S(1)} all-reduce(f32[2048]{0:T(1024)S(1)} %fusion.17), channel_id=1, replica_groups=mesh['gen'=32,'beam'=8] {'gen'}, use_global_device_ids=true, to_apply=%region_23.0 | all-reduce | flops 2048 | bytes 16384 | tf_op jit(solution)/shard_map/pmax | solution.py:29
  464.8 5.2 exponential_reduce_fusion.2
  470.0 63.7 %psum.75 = f32[2048]{0:T(1024)S(1)} all-reduce(f32[2048]{0:T(1024)S(1)} %exponential_reduce_fusion.2), channel_id=1, replica_groups=mesh['gen'=32,'beam'=8] {'gen'}, use_global_device_ids=true, to_apply=%region_25.0 | all-reduce | flops 2048 | bytes 16384 | tf_op jit(solution)/shard_map/psum | solution.py:30
  539.2 16.2 %pmax.62 = f32[1024]{0:T(1024)S(1)} all-reduce(f32[1024]{0:T(1024)S(1)} %fusion.3), channel_id=1, replica_groups=mesh['gen'=32,'beam'=8] {'beam'}, use_global_device_ids=true, to_apply=%region_27.0 | all-reduce | flops 1024 | bytes 8192 | tf_op jit(solution)/shard_map/pmax | solution.py:23
  560.5 14.2 %psum.76 = f32[1024]{0:T(1024)S(1)} all-reduce(f32[1024]{0:T(1024)S(1)} %exponential_reduce_fusion.1), channel_id=1, replica_groups=mesh['gen'=32,'beam'=8] {'beam'}, use_global_device_ids=true, to_apply=%region_29.0 | all-reduce | flops 1024 | bytes 8192 | tf_op jit(solution)/shard_map/psum | solution.py:24
  580.0 63.7 %pmax.63 = f32[2048]{0:T(1024)S(1)} all-reduce(f32[2048]{0:T(1024)S(1)} %fusion.18), channel_id=1, replica_groups=mesh['gen'=32,'beam'=8] {'gen'}, use_global_device_ids=true, to_apply=%region_31.0 | all-reduce | flops 2048 | bytes 16384 | tf_op jit(solution)/shard_map/pmax | solution.py:29
  648.9 63.7 %psum.77 = f32[2048]{0:T(1024)S(1)} all-reduce(f32[2048]{0:T(1024)S(1)} %exponential_reduce_fusion), channel_id=1, replica_groups=mesh['gen'=32,'beam'=8] {'gen'}, use_global_device_ids=true, to_apply=%region_33.0 | all-reduce | flops 2048 | bytes 16384 | tf_op jit(solution)/shard_map/psum | solution.py:30
  713.3 5.7 fusion.37
  728.0 92.3 %reduce-scatter.5.cloned.1.call-done = f32[64,128]{1,0:T(8,128)} async-done(((f32[2048,128]{1,0:T(8,128)}), f32[64,128]{1,0:T(8,128)}) %reduce-scatter.5.cloned.1.call-update) | async-done | bytes 32784 | tf_op jit(solution)/shard_map/reduce_scatter | solution.py:85
  821.3 38.7 %reduce-scatter.3.cloned.1.call-done = f32[128,128]{0,1:T(8,128)} async-done(((f32[1024,128]{0,1:T(8,128)}), f32[128,128]{0,1:T(8,128)}) %reduce-scatter.3.cloned.1.call-update) | async-done | bytes 65552 | tf_op jit(solution)/shard_map/reduce_scatter | solution.py:72
  861.8 109.8 %all-reduce.3.cloned.1.call-done = f32[256,128]{1,0:T(8,128)} async-done(((f32[256,128]{1,0:T(8,128)}), f32[256,128]{1,0:T(8,128)}) %all-reduce.3.cloned.1.call-update) | async-done | bytes 131088 | tf_op jit(solution)/shard_map/psum | solution.py:98
  971.7 74.5 %all-reduce.5.cloned.1.call-done = f32[256,128]{1,0:T(8,128)} async-done(((f32[256,128]{1,0:T(8,128)}), f32[256,128]{1,0:T(8,128)}) %all-reduce.5.cloned.1.call-update) | async-done | bytes 131088 | tf_op jit(solution)/shard_map/psum | solution.py:98
  (45 shorter events, 86.7 us)
Async XLA Ops:
  7.2 1.5 copy-start
  7.2 813.0 %reduce-scatter.5.cloned.1.call-start = ((), (), s32[]{:S(2)}) async-start(), calls=%async_computation.3 | async-start | bytes 1081344 | tf_op jit(solution)/shard_map/reduce_scatter | solution.py:85
  575.4 137.9 %copy-start.2 = (f32[1024]{0:T(1024)}, f32[1024]{0:T(1024)S(1)}, u32[]{:S(2)}) copy-start(f32[1024]{0:T(1024)S(1)} %subtract_multiply_fusion.4) | copy-start | bytes 12292
  713.3 10.0 copy-start.3
  719.0 1.9 copy-start.1
  723.3 136.6 %reduce-scatter.3.cloned.1.call-start = ((), (), s32[]{:S(2)}) async-start(), calls=%async_computation.2 | async-start | bytes 589824 | tf_op jit(solution)/shard_map/reduce_scatter | solution.py:72
  727.9 243.7 %all-reduce.3.cloned.1.call-start = ((), (), s32[]{:S(2)}) async-start(), calls=%async_computation.4 | async-start | bytes 262144 | tf_op jit(solution)/shard_map/psum | solution.py:98
  861.7 184.5 %all-reduce.5.cloned.1.call-start = ((), (), s32[]{:S(2)}) async-start(), calls=%async_computation.5 | async-start | bytes 262144 | tf_op jit(solution)/shard_map/psum | solution.py:98
Sparse Core Ops, SparseCore 0:
  723.5 96.7 reduce-scatter.4
  822.9 36.9 reduce-scatter.2
  863.7 107.8 all-reduce.2
  973.9 72.2 all-reduce.4
